TPU v7x, 32 devices: a whole 2x2x4 slice. The times are simulated.
32 devices in a mesh: run: 2 (over y), tile: 4 (over z), site: 2 (over x), freq: 2 (over core).
Axes of the slice: x: 2, y: 2, z: 4, core: 2. Of those that a mesh axis runs over, the one named last changes fastest.
Arguments:
- jacobian: bfloat16 [256, 16, 8, 8, 128], P(('run', 'tile', 'site'), None, 'freq'), parts along dimension 0, may hold values from -6 to 6
- footprint: int32 [256, 16], P(('run', 'tile', 'site')), parts along dimension 0, may hold values from 0 to 4095, as said below
- home: int32 [8192], P('run'), parts along dimension 0, may hold values from 0 to 4095, as said below
- residual: float32 [256, 8, 8], P(('run', 'tile', 'site'), 'freq'), parts along dimension 0, may hold values from -6 to 6
- weights: float32 [256], P(('run', 'tile', 'site')), parts along dimension 0, may hold values from 0.2 to 2
- damping: float32 [8192, 128], P(('run', 'tile', 'site')), parts along dimension 0, may hold values from 2 to 50
- step_lengths: float32 [8], replicated, may hold values from 0.2 to 1.2
Outputs:
- model_step: float32 [8192, 128], P(('run', 'tile', 'site')), parts along dimension 0
- change: float32 [256, 8, 8], P(('run', 'tile', 'site'), 'freq'), parts along dimension 0
- curve: float32 [16, 8], P(('run', 'freq')), parts along dimension 0
There are 2 independent parts, one for each index of `run`. A program takes and returns all parts, laid end to end along the dimension named above; an argument that names none is the same for every part. Nothing has to cross between parts.
Inputs may be any that keep to these rules, and one draw needn't show every extreme that they name: home is a permutation of 0 to 4095. `footprint`: of the 256 entries of each aligned block of 16 sites, at most 64 have home[block] // 512 equal to any one value; one value receives exactly 64 entries from every such block.
All inputs are finite; a program needn't handle non-finite values.
Results may differ from a plain program's by a relative error of at most 0.0029.
Values may be sent and summed in bfloat16 or wider, within the bound.
A program may use at most 64 MiB of HBM per device.

v0:
```python
import jax
import jax.numpy as jnp
from jax import lax
from jax.sharding import PartitionSpec as P


def shards(jacobian, footprint, home, residual, weights, damping, step_lengths):
    site_count, foot_count, freq_local, comps, width = jacobian.shape
    blocks_dev = damping.shape[0]
    tiles = lax.axis_size("tile")
    groups = lax.axis_size("site")
    owner_count = tiles * groups
    entries = site_count * foot_count
    capacity = 2 * entries // owner_count
    weighted = (weights[:, None, None] * residual).astype(jnp.bfloat16)
    grad_terms = jnp.einsum(
        "skfcb,sfc->skb", jacobian, weighted, preferred_element_type=jnp.float32
    )
    curve_terms = weights[:, None, None] * jnp.sum(
        jnp.square(jacobian.astype(jnp.float32)), axis=(2, 3)
    )
    terms = jnp.concatenate([grad_terms, curve_terms], axis=-1).reshape(entries, 2 * width)
    position = home[footprint.reshape(-1)]
    dest_rank = position // blocks_dev
    local_slot = position % blocks_dev
    member = (dest_rank[:, None] == jnp.arange(owner_count, dtype=jnp.int32)[None, :]).astype(
        jnp.int32
    )
    earlier = jnp.cumsum(member, axis=0) - member
    order_in = jnp.sum(earlier * member, axis=1)
    bucket = dest_rank * capacity + order_in
    outgoing = jnp.zeros((owner_count * capacity, 2 * width), jnp.float32).at[bucket].set(terms)
    out_slots = (
        jnp.full((owner_count * capacity,), blocks_dev, jnp.int32).at[bucket].set(local_slot)
    )
    received, in_slots = (
        lax.all_to_all(
            outgoing.reshape(owner_count, capacity, 2 * width),
            ("tile", "site"),
            split_axis=0,
            concat_axis=0,
            tiled=True,
        ),
        lax.all_to_all(
            out_slots.reshape(owner_count, capacity),
            ("tile", "site"),
            split_axis=0,
            concat_axis=0,
            tiled=True,
        ),
    )
    flat_slots = in_slots.reshape(-1)
    totals = jax.ops.segment_sum(
        received.reshape(-1, 2 * width), flat_slots, num_segments=blocks_dev + 1
    )[:blocks_dev]
    totals = lax.psum(totals, "freq")
    model_step = totals[:, :width] / (totals[:, width:] + damping)
    step_low = jnp.concatenate(
        [model_step.astype(jnp.bfloat16), jnp.zeros((1, width), jnp.bfloat16)], axis=0
    )
    reply = step_low[flat_slots]
    returned = lax.all_to_all(
        reply.reshape(owner_count, capacity, width),
        ("tile", "site"),
        split_axis=0,
        concat_axis=0,
        tiled=True,
    )
    entry_rows = returned.reshape(owner_count * capacity, width)[bucket]
    entry_step = entry_rows.reshape(site_count, foot_count, width)
    change = jnp.einsum("skfcb,skb->sfc", jacobian, entry_step, preferred_element_type=jnp.float32)
    scale_total = site_count * owner_count * comps
    gap = residual[:, :, :, None] - step_lengths[None, None, None, :] * change[:, :, :, None]
    partial_sum = jnp.einsum("s,sfca->fa", weights, gap * gap)
    curve = lax.psum(partial_sum, ("tile", "site")) / scale_total
    return (model_step, change, curve)


def solution(mesh):
    placed = (
        P(("run", "tile", "site"), None, "freq", None, None),
        P(("run", "tile", "site"), None),
        P("run"),
        P(("run", "tile", "site"), "freq", None),
        P(("run", "tile", "site")),
        P(("run", "tile", "site"), None),
        P(),
    )
    return jax.shard_map(
        shards,
        mesh=mesh,
        in_specs=placed,
        out_specs=(
            P(("run", "tile", "site"), None),
            P(("run", "tile", "site"), "freq", None),
            P(("run", "freq"), None),
        ),
        check_vma=False,
    )
```

profile of v0, /device:TPU:0, one launch (start us, length us, event | category | flops | bytes accessed | tf_op | source)
XLA Modules:
  0.0 117.0 jit_solution(13052791357690887810)
XLA Ops:
  7.2 0.0 copy-start
  7.2 0.0 copy-start.1
  7.2 0.0 copy-start.5
  7.2 0.0 copy-start.4
  7.2 0.9 reshape.181
  8.2 0.0 copy-done
  8.2 1.7 %gather_fusion = s32[256]{0:T(256)S(1)} fusion(s32[4096]{0:T(1024)S(1)} %copy-done, s32[1024]{0:T(1024)S(1)} %pad_clamp_fusion.2), kind=kCustom, calls=%fused_computation | custom fusion | bytes 3072 | tf_op jit(solution)/shard_map/gather | solution.py:23
  9.9 0.6 reduce-window.6
  10.5 0.2 slice_reduce_fusion
  10.8 0.1 fusion.10
  10.9 1.4 %scatter_custom_fusion = s32[512]{0:T(512)S(1)} fusion(s32[256]{0:T(256)S(1)} %bitcast.64, s32[256]{0:T(256)S(1)} %get-tuple-element.5, s32[]{:T(128)} %constant.41.clone.1), kind=kCustom, calls=%fused_computation.49 | custom fusion | bytes 2052 | tf_op jit(solution)/shard_map/scatter | solution.py:34
  12.3 0.7 all_to_all.12
  13.0 7.3 %all-to-all-start = ((s32[8,1,64]{2,1,0:T(1,128)}), s32[8,1,64]{2,1,0:T(1,128)S(1)}, u32[]{:S(2)}, u32[]{:S(2)}) async-start(s32[8,1,64]{2,1,0:T(1,128)} %all_to_all.12), calls=%async_computation | async-start | bytes 8192 | tf_op jit(solution)/shard_map/all_to_all | solution.py:44
  20.2 2.3 %multiply_reduce_fusion = f32[16,16,128]{2,1,0:T(8,128)S(1)} fusion(bf16[16,16,4,8,128]{4,3,2,1,0:T(8,128)(2,1)} %param.7), kind=kLoop, calls=%fused_computation.6 | loop fusion | flops 3112960 | bytes 2228224 | tf_op jit(solution)/shard_map/reduce_sum | solution.py:19
  22.6 0.0 copy-done.5
  22.6 0.1 broadcast_multiply_fusion
  22.7 0.0 copy-done.4
  22.7 0.1 copy.14
  22.8 0.0 copy-done.1
  22.8 0.6 fusion.22
  23.4 0.0 copy-start.2
  23.4 2.2 %scatter_custom_fusion.1 = f32[512,256]{1,0:T(8,128)} fusion(s32[256]{0:T(256)S(1)} %bitcast.65, f32[256,256]{1,0:T(8,128)S(1)} %bitcast.56, f32[]{:T(128)} %constant.40.clone.1), kind=kCustom, calls=%fused_computation.14 | custom fusion | bytes 524292 | tf_op jit(solution)/shard_map/scatter | solution.py:32
  25.6 1.0 all-to-all-done
  26.6 5.0 %all-to-all-start.1 = ((f32[8,64,256]{2,1,0:T(8,128)}), f32[8,64,256]{2,1,0:T(8,128)S(1)}, u32[]{:S(2)}, u32[]{:S(2)}) async-start(f32[8,64,256]{2,1,0:T(8,128)} %bitcast.11), calls=%async_computation.1 | async-start | bytes 1048576 | tf_op jit(solution)/shard_map/all_to_all | solution.py:37
  31.6 0.0 all-reduce.3.cloned.1.call-start
  31.7 0.5 broadcast.204
  32.2 0.7 reduce.7
  32.8 0.1 reshape.231
  32.9 12.7 %all-to-all-done.1 = f32[8,64,256]{2,1,0:T(8,128)S(1)} async-done(((f32[8,64,256]{2,1,0:T(8,128)}), f32[8,64,256]{2,1,0:T(8,128)S(1)}, u32[]{:S(2)}, u32[]{:S(2)}) %all-to-all-start.1) | async-done | bytes 524320 | tf_op jit(solution)/shard_map/all_to_all | solution.py:37
  45.6 3.7 %scatter_custom_fusion.2 = f32[513,256]{1,0:T(8,128)S(1)} fusion(s32[512]{0:T(512)S(1)} %reshape.231, f32[512,256]{1,0:T(8,128)S(1)} %bitcast.54, f32[]{:T(128)} %constant.40.clone.1), kind=kCustom, calls=%fused_computation.9 | custom fusion | flops 131072 | bytes 525316 | tf_op jit(solution)/shard_map/scatter-add | solution.py:53
  49.3 0.8 slice.27
  50.1 0.0 all-reduce.3.cloned.1.call-update
  50.1 0.1 broadcast_in_dim_reshape.3
  50.2 17.9 %all-reduce.3.cloned.1.call-done = f32[512,256]{1,0:T(8,128)} async-done(((f32[512,256]{1,0:T(8,128)}), f32[512,256]{1,0:T(8,128)}) %all-reduce.3.cloned.1.call-update) | async-done | bytes 524304 | tf_op jit(solution)/shard_map/psum | solution.py:56
  68.1 0.0 copy-done.2
  68.1 1.8 %fusion.17 = (bf16[512,128]{1,0:T(8,128)(2,1)S(1)}, f32[512,128]{1,0:T(8,128)}) fusion(f32[512,128]{1,0:T(8,128)S(1)} %copy-done.2, f32[512,256]{1,0:T(8,128)} %all-reduce.3.cloned.1.call-done), kind=kLoop, calls=%fused_computation.55 | loop fusion | flops 196608 | bytes 1179648 | tf_op jit(solution)/shard_map/convert_element_type | solution.py:59
  70.0 1.9 %gather_fusion.1 = bf16[512,128]{1,0:T(8,128)(2,1)} fusion(bf16[513,128]{1,0:T(8,128)(2,1)S(1)} %concatenate.7, s32[1024]{0:T(1024)S(1)} %pad_clamp_fusion.1), kind=kCustom, calls=%fused_computation.1 | custom fusion | bytes 264192 | tf_op jit(solution)/shard_map/gather | solution.py:61
  71.9 5.8 %all-to-all-start.2 = ((bf16[8,64,128]{2,1,0:T(8,128)(2,1)}), bf16[8,64,128]{2,1,0:T(8,128)(2,1)S(1)}, u32[]{:S(2)}, u32[]{:S(2)}) async-start(bf16[8,64,128]{2,1,0:T(8,128)(2,1)} %bitcast.14), calls=%async_computation.2 | async-start | bytes 262144 | tf_op jit(solution)/shard_map/all_to_all | solution.py:62
  77.7 7.4 %all-to-all-done.2 = bf16[8,64,128]{2,1,0:T(8,128)(2,1)S(1)} async-done(((bf16[8,64,128]{2,1,0:T(8,128)(2,1)}), bf16[8,64,128]{2,1,0:T(8,128)(2,1)S(1)}, u32[]{:S(2)}, u32[]{:S(2)}) %all-to-all-start.2) | async-done | bytes 131104 | tf_op jit(solution)/shard_map/all_to_all | solution.py:62
  85.1 0.0 copy-start.6
  85.1 0.9 gather_fusion.2
  85.9 4.7 %fusion = f32[16,1,4,8,1]{3,1,4,2,0:T(1,128)S(1)} fusion(bf16[16,16,4,8,128]{4,3,2,1,0:T(8,128)(2,1)S(1)} %copy-done.1, bf16[16,16,128,1,1]{2,1,0,3,4:T(8,128)(2,1)S(1)} %bitcast.57), kind=kOutput, calls=%fused_computation.7 | convolution fusion | flops 2097152 | bytes 2164736 | tf_op jit(solution)/shard_map/skfcb,skb->sfc/dot_general | solution.py:71
  90.6 0.1 copy.18
  90.7 0.0 copy-start.3
  90.7 0.0 copy-done.6
  90.7 0.1 multiply_reduce_fusion.1
  90.8 0.1 fusion.19
  91.0 18.6 %psum.15 = f32[4,8]{1,0:T(4,128)S(1)} all-reduce(f32[4,8]{1,0:T(4,128)S(1)} %bitcast.63), channel_id=1, replica_groups=mesh['run'=2,'tile'=4,'site'=2,'freq'=2] {'tile','site'}, use_global_device_ids=true, to_apply=%region_9.10 | all-reduce | flops 32 | bytes 256 | tf_op jit(solution)/shard_map/psum | solution.py:75
  109.5 0.6 broadcast_multiply_fusion.1
  110.1 0.0 copy-done.3
  (14 shorter events, 0.2 us)
Async XLA Ops:
  7.2 1.0 copy-start
  7.2 15.6 %copy-start.1 = (bf16[16,16,4,8,128]{4,3,2,1,0:T(8,128)(2,1)S(1)}, bf16[16,16,4,8,128]{4,3,2,1,0:T(8,128)(2,1)}, u32[]{:S(2)}) copy-start(bf16[16,16,4,8,128]{4,3,2,1,0:T(8,128)(2,1)} %param.7) | copy-start | bytes 6291460
  7.2 15.4 %copy-start.5 = (f32[16]{0:T(128)S(1)}, f32[16]{0:T(128)}, u32[]{:S(2)}) copy-start(f32[16]{0:T(128)} %param.11) | copy-start | bytes 196
  7.2 15.5 %copy-start.4 = (f32[16,4,8]{0,2,1:T(8,128)S(1)}, f32[16,4,8]{0,2,1:T(8,128)}, u32[]{:S(2)}) copy-start(f32[16,4,8]{0,2,1:T(8,128)} %param.10) | copy-start | bytes 6148
  13.0 13.6 %all-to-all-start = ((s32[8,1,64]{2,1,0:T(1,128)}), s32[8,1,64]{2,1,0:T(1,128)S(1)}, u32[]{:S(2)}, u32[]{:S(2)}) async-start(s32[8,1,64]{2,1,0:T(1,128)} %all_to_all.12), calls=%async_computation | async-start | bytes 8192 | tf_op jit(solution)/shard_map/all_to_all | solution.py:44
  23.4 44.8 %copy-start.2 = (f32[512,128]{1,0:T(8,128)S(1)}, f32[512,128]{1,0:T(8,128)}, u32[]{:S(2)}) copy-start(f32[512,128]{1,0:T(8,128)} %param.12) | copy-start | bytes 786436
  26.6 19.0 %all-to-all-start.1 = ((f32[8,64,256]{2,1,0:T(8,128)}), f32[8,64,256]{2,1,0:T(8,128)S(1)}, u32[]{:S(2)}, u32[]{:S(2)}) async-start(f32[8,64,256]{2,1,0:T(8,128)} %bitcast.11), calls=%async_computation.1 | async-start | bytes 1048576 | tf_op jit(solution)/shard_map/all_to_all | solution.py:37
  31.6 36.5 %all-reduce.3.cloned.1.call-start = ((), (), s32[]{:S(2)}) async-start(), calls=%async_computation.3 | async-start | bytes 1048576 | tf_op jit(solution)/shard_map/psum | solution.py:56
  71.9 13.2 %all-to-all-start.2 = ((bf16[8,64,128]{2,1,0:T(8,128)(2,1)}), bf16[8,64,128]{2,1,0:T(8,128)(2,1)S(1)}, u32[]{:S(2)}, u32[]{:S(2)}) async-start(bf16[8,64,128]{2,1,0:T(8,128)(2,1)} %bitcast.14), calls=%async_computation.2 | async-start | bytes 262144 | tf_op jit(solution)/shard_map/all_to_all | solution.py:62
  85.1 5.6 %copy-start.6 = (f32[8]{0:T(128)S(1)}, f32[8]{0:T(128)}, u32[]{:S(2)}) copy-start(f32[8]{0:T(128)} %param.13) | copy-start | bytes 100
  90.7 19.4 %copy-start.3 = (f32[16,1,4,8,1]{0,3,2,1,4:T(8,128)}, f32[16,1,4,8,1]{0,3,2,1,4:T(8,128)S(1)}, u32[]{:S(2)}) copy-start(f32[16,1,4,8,1]{0,3,2,1,4:T(8,128)S(1)} %copy.18) | copy-start | bytes 6148
Sparse Core Ops, SparseCore 0:
  50.3 17.8 all-reduce.2
where the time goes:
time: 117 us
  waiting for transfers between devices  39 us (33%)
  blocking collectives  18.6 us (16%)
  starting transfers between devices  18.1 us (15%)
  between operations  14.2 us (12%)
  local copies, waits for them, and re-layouts  11.6 us (10%)
  other arithmetic  10.1 us (9%)
  matrix products  5.41 us (5%)
    psum x1, blocking collectives, shards(): curve = lax.psum(partial_sum, ('tile', 'site')) / scale_total  18.6 us
    psum x1, waiting for transfers between devices, shards(): totals = lax.psum(totals, 'freq')  17.9 us
    all_to_all x1, waiting for transfers between devices, shards(): lax.all_to_all(outgoing.reshape(owner_count, capacity, 2 * width), ('tile...  12.7 us
    all_to_all x1, waiting for transfers between devices, shards(): lax.all_to_all(reply.reshape(owner_count, capacity, width), ('tile', 'sit...  7.43 us
    all_to_all x1, starting transfers between devices, shards(): lax.all_to_all(out_slots.reshape(owner_count, capacity), ('tile', 'site')...  7.25 us
    all_to_all x1, starting transfers between devices, shards(): lax.all_to_all(reply.reshape(owner_count, capacity, width), ('tile', 'sit...  5.78 us
    all_to_all x1, starting transfers between devices, shards(): lax.all_to_all(outgoing.reshape(owner_count, capacity, 2 * width), ('tile...  5 us
    dot_general x1, matrix products, shards(): jnp.einsum('skfcb,skb->sfc', jacobian, entry_step, preferred_element_type...  4.69 us
  transfers between devices with their start and end apart: 4, of which 4 were waited for; matrix products, arithmetic and copies ran while one was open for 6% of the time, Pallas kernels for 0%

commit v1 on v0

v1 whole, which is shorter than its diff:
```python
import functools

import jax
import jax.numpy as jnp
from jax import lax
from jax.experimental import pallas as pl
from jax.experimental.pallas import tpu as pltpu
from jax.sharding import PartitionSpec as P

MESH = pl.DeviceIdType.MESH
F32, BF16, I32 = jnp.float32, jnp.bfloat16, jnp.int32
LANES = 128
PIECES = 4


def count(shape, dim):
    return lax.broadcasted_iota(I32, shape, dim)


def diagonal(rows, columns):
    return count((rows, columns), 0) == count((rows, columns), 1)


def column_of(row, rows):
    wide = jnp.broadcast_to(row, (rows, row.shape[1]))
    return jnp.sum(jnp.where(diagonal(*wide.shape), wide, 0.0), axis=1, keepdims=True)


def row_of(column, columns):
    wide = jnp.broadcast_to(column, (column.shape[0], columns))
    return jnp.sum(jnp.where(diagonal(*wide.shape), wide, 0.0), axis=0, keepdims=True)


def one_hot(mask):
    return jnp.where(mask, 1.0, 0.0).astype(BF16)


def dot(a, b):
    return jnp.dot(a, b, preferred_element_type=F32)


def kernel(
    sizes,
    jac_any, foot_ref, home_ref, res_ref, w_ref, damp_any, len_ref,
    step_any, change_ref, curve_ref,
    jac, damp, terms, other, split, pick, pick_t, slot_out, slot_in, put, put_t,
    out, inn, both, step, low, rep, ret, entry, curves,
    load_sem, damp_sem, step_sem, pair_sem, total_sem, slot_sem, out_sem, rep_sem, curve_sem,
):
    n, groups, cap, sites, foot, freqs, comps, blocks = sizes
    entries = sites * foot
    rows = n * cap
    run, tile, site, freq = (lax.axis_index(a) for a in ("run", "tile", "site", "freq"))
    me = tile * groups + site
    partner = (run, tile, site, 1 - freq)

    def at(o):
        return (run, o // groups, o % groups, freq)

    def others(body):
        def one(j, carry):
            body((me + j) % n)
            return carry
        lax.fori_loop(1, n, one, 0)

    def place(o):
        return pl.ds(pl.multiple_of(o * cap, cap), cap)

    def remote(src, dst, sems, send, recv, to):
        return pltpu.make_async_remote_copy(
            src_ref=src, dst_ref=dst, send_sem=sems.at[0, send], recv_sem=sems.at[1, recv],
            device_id=to, device_id_type=MESH,
        )

    piece = entries // PIECES
    loads = [
        pltpu.make_async_copy(
            jac_any.at[pl.ds(c * piece, piece)], jac.at[pl.ds(c * piece, piece)], load_sem.at[c]
        )
        for c in range(PIECES)
    ]
    for load in loads:
        load.start()
    damp_load = pltpu.make_async_copy(damp_any, damp, damp_sem)
    damp_load.start()
    barrier = pltpu.get_barrier_semaphore()
    pl.semaphore_signal(barrier, inc=1, device_id=partner, device_id_type=MESH)
    others(
        lambda o: pl.semaphore_signal(barrier, inc=1, device_id=at(o), device_id_type=MESH)
    )

    block = jnp.concatenate(
        [column_of(foot_ref[s : s + 1, :].astype(F32), foot) for s in range(sites)], axis=0
    ).astype(I32)
    home = home_ref[...]
    line = one_hot(count((entries, home.shape[0]), 1) == (block >> 7))
    found = dot(line, (home & 255).astype(F32).astype(BF16)) + 256.0 * dot(
        line, (home >> 8).astype(F32).astype(BF16)
    )
    here = count((entries, LANES), 1) == (block & 127)
    position = jnp.sum(jnp.where(here, found, 0.0), axis=1, keepdims=True)
    wide = -(-n // LANES) * LANES
    owner = count((entries, wide), 1).astype(F32)
    first = owner * float(blocks)
    member = jnp.where((position >= first) & (position < first + float(blocks)), 1.0, 0.0)
    lower = one_hot(count((entries, entries), 0) > count((entries, entries), 1))
    earlier = dot(lower, member.astype(BF16))
    bucket = jnp.sum(member * (earlier + owner * float(cap)), axis=1, keepdims=True)
    slot = position - jnp.sum(member * first, axis=1, keepdims=True)
    pick_t[...] = one_hot(bucket == count((entries, rows), 1).astype(F32))
    pick[...] = one_hot(row_of(bucket, entries) == count((rows, entries), 0).astype(F32))
    lane = count((entries, LANES), 1) - (me * cap) % LANES
    inside = (lane >= 0) & (lane < cap)
    lane = lane.astype(F32)

    def list_slots(o, carry):
        hit = inside & (bucket - (o * cap).astype(F32) == lane)
        slots = jnp.sum(jnp.where(hit, slot, 0.0), axis=0, keepdims=True)
        slot_out[o] = jnp.broadcast_to(slots, (8, LANES))
        return carry

    lax.fori_loop(0, n, list_slots, 0)
    slot_in[me] = slot_out[me]

    pl.semaphore_wait(barrier, n)

    def slot_copy(o, source):
        return remote(slot_out.at[o], slot_in.at[source], slot_sem, o, source, at(o))

    others(lambda o: slot_copy(o, me).start())

    def pair_copy(c):
        span = pl.ds(c * piece, piece)
        return remote(terms.at[1 - freq, span], other.at[span], pair_sem, c, c, partner)

    def site_terms(s, carry):
        w = w_ref[s]
        weighted = jnp.concatenate(
            [
                column_of((res_ref[s, f : f + 1, :] * w).astype(BF16).astype(F32), comps)
                for f in range(freqs)
            ],
            axis=0,
        )
        span = pl.ds(pl.multiple_of(s * foot, foot), foot)
        j = jac[span].astype(F32)
        terms[0, span, :] = jnp.sum(j * weighted[None], axis=1)
        terms[1, span, :] = jnp.sum(j * j, axis=1) * w
        return carry

    for c in range(PIECES):
        loads[c].wait()
        lax.fori_loop(c * sites // PIECES, (c + 1) * sites // PIECES, site_terms, 0)
        pair_copy(c).start()
    for c in range(PIECES):
        span = pl.ds(c * piece, piece)
        pair_copy(c).wait_recv()
        t = terms[freq, span, :] + other[span, :]
        high = t.astype(BF16)
        split[span, :LANES] = high
        split[span, LANES:] = (t - high.astype(F32)).astype(BF16)

    def bucket_rows(o):
        return dot(pick[place(o), :], split[...]).astype(BF16)

    def out_copy(o, source):
        return remote(out.at[o], inn.at[place(source)], out_sem, o, source, at(o))

    def send_out(o):
        out[o] = bucket_rows(o)
        out_copy(o, me).start()

    others(send_out)
    inn[place(me), :] = bucket_rows(me)

    others(lambda o: slot_copy(o, o).wait_recv())
    per = LANES // cap
    for g in range(rows // LANES):
        listed = slot_in[g * per, 0:1, :]
        for p in range(1, per):
            listed = listed + slot_in[g * per + p, 0:1, :]
        span = slice(g * LANES, (g + 1) * LANES)
        put[:, span] = one_hot(listed == count((blocks, LANES), 0).astype(F32))
        put_t[span, :] = one_hot(
            column_of(listed, LANES) == count((LANES, blocks), 1).astype(F32)
        )

    others(lambda o: out_copy(o, o).wait_recv())
    part = blocks // PIECES

    def total_copy(c):
        span = pl.ds(c * part, part)
        return remote(both.at[freq, span], both.at[freq, span], total_sem, c, c, partner)

    for c in range(PIECES):
        t = dot(put[c * part : (c + 1) * part, :], inn[...])
        both[freq, pl.ds(c * part, part), :] = t[:, :LANES] + t[:, LANES:]
        total_copy(c).start()
    damp_load.wait()
    for c in range(PIECES):
        span = pl.ds(c * part, part)
        total_copy(c).wait_recv()
        update = both[0, span, :] / (both[1, span, :] + damp[span, :])
        step[span, :] = update
        low[span, :] = update.astype(BF16)
    step_store = pltpu.make_async_copy(step, step_any, step_sem)
    step_store.start()

    def reply_rows(o):
        return dot(put_t[place(o), :], low[...]).astype(BF16)

    def rep_copy(o, source):
        return remote(rep.at[o], ret.at[place(source)], rep_sem, o, source, at(o))

    def send_reply(o):
        rep[o] = reply_rows(o)
        rep_copy(o, me).start()

    others(send_reply)
    ret[place(me), :] = reply_rows(me)
    others(lambda o: rep_copy(o, o).wait_recv())
    entry[...] = dot(pick_t[...], ret[...])

    steps = len_ref.shape[0]
    eye = diagonal(comps, LANES)

    def site_change(s, sums):
        acc = jnp.zeros((freqs * comps, LANES), F32)
        for k in range(foot):
            e = s * foot + k
            acc = acc + jac[e].astype(F32) * entry[pl.ds(e, 1), :]
        total = jnp.sum(acc, axis=1, keepdims=True)
        ch = jnp.concatenate(
            [
                jnp.sum(
                    jnp.where(eye, total[f * comps : (f + 1) * comps], 0.0), axis=0, keepdims=True
                )
                for f in range(freqs)
            ],
            axis=0,
        )[:, :comps]
        change_ref[s] = ch
        r, w = res_ref[s], w_ref[s]
        gaps = [r - len_ref[a] * ch for a in range(steps)]
        return tuple(t + w * (g * g) for t, g in zip(sums, gaps))

    zero = jnp.zeros((freqs, comps), F32)
    sums = lax.fori_loop(0, sites, site_change, (zero,) * steps)
    mine = jnp.zeros((freqs, LANES), F32)
    for a in range(steps):
        here = count((freqs, LANES), 1) == a
        mine = mine + jnp.where(here, jnp.sum(sums[a], axis=1, keepdims=True), 0.0)
    curves[me] = jnp.zeros((8, LANES), F32)
    curves[me, :freqs, :] = mine

    def curve_copy(o, source):
        return remote(curves.at[me], curves.at[source], curve_sem, o, source, at(o))

    others(lambda o: curve_copy(o, me).start())
    others(lambda o: curve_copy(o, o).wait_recv())
    total = lax.fori_loop(
        0, n, lambda i, t: t + curves[i], jnp.zeros((8, LANES), F32)
    )
    curve_ref[...] = total[:freqs, :steps] * (1.0 / (n * sites * comps))

    for c in range(PIECES):
        pair_copy(c).wait_send()
        total_copy(c).wait_send()
    others(lambda o: slot_copy(o, me).wait_send())
    others(lambda o: out_copy(o, me).wait_send())
    others(lambda o: rep_copy(o, me).wait_send())
    others(lambda o: curve_copy(o, me).wait_send())
    step_store.wait()


def shards(jacobian, footprint, home, residual, weights, damping, step_lengths):
    sites, foot, freqs, comps, width = jacobian.shape
    blocks = damping.shape[0]
    groups = lax.axis_size("site")
    n = lax.axis_size("tile") * groups
    entries = sites * foot
    cap = 16
    while cap < 2 * entries // n:
        cap *= 2
    rows = n * cap
    sizes = (n, groups, cap, sites, foot, freqs, comps, blocks)
    vmem = pl.BlockSpec(memory_space=pltpu.VMEM)
    smem = pl.BlockSpec(memory_space=pltpu.SMEM)
    hbm = pl.BlockSpec(memory_space=pl.ANY)
    dma = pltpu.SemaphoreType.DMA
    return pl.pallas_call(
        functools.partial(kernel, sizes),
        out_shape=(
            jax.ShapeDtypeStruct((blocks, width), F32),
            jax.ShapeDtypeStruct((sites, freqs, comps), F32),
            jax.ShapeDtypeStruct((freqs, step_lengths.shape[0]), F32),
        ),
        in_specs=[hbm, vmem, vmem, vmem, smem, hbm, smem],
        out_specs=(hbm, vmem, vmem),
        scratch_shapes=[
            pltpu.VMEM((entries, freqs * comps, width), BF16),
            pltpu.VMEM((blocks, width), F32),
            pltpu.VMEM((2, entries, width), F32),
            pltpu.VMEM((entries, width), F32),
            pltpu.VMEM((entries, 2 * width), BF16),
            pltpu.VMEM((rows, entries), BF16),
            pltpu.VMEM((entries, rows), BF16),
            pltpu.VMEM((n, 8, LANES), F32),
            pltpu.VMEM((n, 8, LANES), F32),
            pltpu.VMEM((blocks, rows), BF16),
            pltpu.VMEM((rows, blocks), BF16),
            pltpu.VMEM((n, cap, 2 * width), BF16),
            pltpu.VMEM((rows, 2 * width), BF16),
            pltpu.VMEM((2, blocks, width), F32),
            pltpu.VMEM((blocks, width), F32),
            pltpu.VMEM((blocks, width), BF16),
            pltpu.VMEM((n, cap, width), BF16),
            pltpu.VMEM((rows, width), BF16),
            pltpu.VMEM((entries, width), F32),
            pltpu.VMEM((n, 8, LANES), F32),
            dma((PIECES,)),
            dma,
            dma,
            dma((2, PIECES)),
            dma((2, PIECES)),
            dma((2, n)),
            dma((2, n)),
            dma((2, n)),
            dma((2, n)),
        ],
        compiler_params=pltpu.CompilerParams(
            collective_id=0, has_side_effects=True, vmem_limit_bytes=48 * 1024 * 1024
        ),
    )(
        jacobian.reshape(entries, freqs * comps, width),
        footprint,
        home.reshape(-1, LANES),
        residual,
        weights,
        damping,
        step_lengths,
    )


def solution(mesh):
    placed = (
        P(("run", "tile", "site"), None, "freq", None, None),
        P(("run", "tile", "site"), None),
        P("run"),
        P(("run", "tile", "site"), "freq", None),
        P(("run", "tile", "site")),
        P(("run", "tile", "site"), None),
        P(),
    )
    return jax.shard_map(
        shards,
        mesh=mesh,
        in_specs=placed,
        out_specs=(
            P(("run", "tile", "site"), None),
            P(("run", "tile", "site"), "freq", None),
            P(("run", "freq"), None),
        ),
        check_vma=False,
    )
```

time: 117 us -> 42.7 us (0.36)
  waiting for transfers between devices: 39 us -> 0 us
  Pallas kernels: 0 us -> 33.7 us
  blocking collectives: 18.6 us -> 0 us
  starting transfers between devices: 18.1 us -> 0 us
  between operations: 14.2 us -> 0.65 us
  other arithmetic: 10.1 us -> 0 us
  matrix products: 5.41 us -> 0 us
  local copies, waits for them, and re-layouts: 11.6 us -> 8.03 us
    pallas_call x0 -> x1, Pallas kernels: none -> 33.7 us  [shards(): pl.pallas_call(functools.partial(kernel, sizes), out_shape=(jax.ShapeDtyp...]
    all_to_all x3 -> x0, waiting for transfers between devices: 21.1 us -> none  [the longest x1 12.7 us: shards(): lax.all_to_all(outgoing.reshape(owner_count, capacity, 2 * width), ('tile...]
    psum x1 -> x0, blocking collectives: 18.6 us -> none  [shards(): curve = lax.psum(partial_sum, ('tile', 'site')) / scale_total]
    all_to_all x3 -> x0, starting transfers between devices: 18 us -> none  [the longest x1 7.25 us: shards(): lax.all_to_all(out_slots.reshape(owner_count, capacity), ('tile', 'site')...]
    psum x1 -> x0, waiting for transfers between devices: 17.9 us -> none  [shards(): totals = lax.psum(totals, 'freq')]
    unnamed x14 -> x15, local copies, waits for them, and re-layouts: 0.04 us -> 7.34 us
    dot_general x3 -> x0, matrix products: 5.41 us -> none  [the longest x1 4.69 us: shards(): jnp.einsum('skfcb,skb->sfc', jacobian, entry_step, preferred_element_type...]
    gather x3 -> x0, local copies, waits for them, and re-layouts: 4.48 us -> none  [the longest x1 1.9 us: shards(): reply = step_low[flat_slots]]
  transfers between devices with their start and end apart: 4 -> 0, of which waited for: 4 -> 0; matrix products, arithmetic and copies ran while one was open for 6% -> 0% of each run, Pallas kernels for 0% -> 0%
where the time goes in v1:
time: 42.7 us; the launch traced here: 42.3 us
  Pallas kernels  33.7 us (79%)
  local copies, waits for them, and re-layouts  8.03 us (19%)
  between operations  0.65 us (2%)
    pallas_call x1, Pallas kernels, shards(): pl.pallas_call(functools.partial(kernel, sizes), out_shape=(jax.ShapeDtyp...  33.7 us
    unnamed x15, local copies, waits for them, and re-layouts  7.34 us

profile of v1, /device:TPU:0, one launch (start us, length us, event | category | flops | bytes accessed | tf_op | source)
XLA Modules:
  0.0 42.3 jit_solution(10659162255069288848)
XLA Ops:
  0.6 0.8 %copy.10.res_ref = f32[16,4,8]{2,1,0:T(4,128)S(1)} copy(f32[16,4,8]{0,2,1:T(8,128)} %param.10) | data formatting | bytes 4096 | tf_op args[3]
  1.4 0.0 copy-start
  1.4 1.6 %copy-done = bf16[16,16,4,8,128]{4,3,2,1,0:T(8,128)(2,1)S(1)} copy-done((bf16[16,16,4,8,128]{4,3,2,1,0:T(8,128)(2,1)S(1)}, bf16[16,16,4,8,128]{4,3,2,1,0:T(8,128)(2,1)}, u32[]{:S(2)}) %copy-start) | copy-done | bytes 2097176
  3.0 0.0 copy-start.1
  3.0 0.9 %copy-done.1 = f32[512,128]{1,0:T(8,128)S(1)} copy-done((f32[512,128]{1,0:T(8,128)S(1)}, f32[512,128]{1,0:T(8,128)}, u32[]{:S(2)}) %copy-start.1) | copy-done | bytes 262168
  4.0 0.0 copy-start.2
  4.0 0.7 %copy-done.2 = s32[4096]{0:T(1024)S(1)} copy-done((s32[4096]{0:T(1024)S(1)}, s32[4096]{0:T(1024)}, u32[]{:S(2)}) %copy-start.2) | copy-done | bytes 16408
  4.7 0.0 copy-start.3
  4.7 0.7 %copy-done.3 = s32[16,16]{1,0:T(8,128)S(1)} copy-done((s32[16,16]{1,0:T(8,128)S(1)}, s32[16,16]{1,0:T(8,128)}, u32[]{:S(2)}) %copy-start.3) | copy-done | bytes 1048
  5.4 0.0 copy-start.4
  5.4 0.7 %copy-done.4 = f32[16]{0:T(128)S(1)} copy-done((f32[16]{0:T(128)S(1)}, f32[16]{0:T(128)}, u32[]{:S(2)}) %copy-start.4) | copy-done | bytes 88
  6.0 0.0 copy-start.5
  6.0 0.7 %copy-done.5 = f32[8]{0:T(128)S(1)} copy-done((f32[8]{0:T(128)S(1)}, f32[8]{0:T(128)}, u32[]{:S(2)}) %copy-start.5) | copy-done | bytes 56
  6.7 33.7 %shard_map.94 = (f32[512,128]{1,0:T(8,128)S(1)}, f32[16,4,8]{2,1,0:T(4,128)S(1)}, f32[4,8]{1,0:T(4,128)S(1)}) custom-call(bf16[256,32,128]{2,1,0:T(8,128)(2,1)S(1)} %bitcast.2, s32[16,16]{1,0:T(8,128)S(1)} %copy-done.3, s32[32,128]{1,0:T(8,128)S(1)} %bitcast.3, f32[16,4,8]{2,1,0:T(4,128)S(1)} %copy.10.res_ref, f32[16]{0:T(128)S(1)} %copy-done.4, ...), custom_call_target="tpu_custom_call" | custom-call | tf_op jit(solution)/shard_map/pallas_call | solution.py:291
  40.4 0.7 %copy.11 = f32[16,4,8]{0,2,1:T(8,128)} copy(f32[16,4,8]{2,1,0:T(4,128)S(1)} %get-tuple-element.4) | data formatting | bytes 4096 | tf_op jit(solution)/shard_map/pallas_call | solution.py:291
  41.0 0.7 %copy.14 = f32[512,128]{1,0:T(8,128)} copy(f32[512,128]{1,0:T(8,128)S(1)} %get-tuple-element.9) | data formatting | bytes 524288
  41.8 0.6 %copy.15 = f32[4,8]{1,0:T(4,128)} copy(f32[4,8]{1,0:T(4,128)S(1)} %get-tuple-element.11) | data formatting | bytes 256
Async XLA Ops:
  1.4 1.6 %copy-start = (bf16[16,16,4,8,128]{4,3,2,1,0:T(8,128)(2,1)S(1)}, bf16[16,16,4,8,128]{4,3,2,1,0:T(8,128)(2,1)}, u32[]{:S(2)}) copy-start(bf16[16,16,4,8,128]{4,3,2,1,0:T(8,128)(2,1)} %param.7) | copy-start | bytes 6291460
  3.0 0.9 %copy-start.1 = (f32[512,128]{1,0:T(8,128)S(1)}, f32[512,128]{1,0:T(8,128)}, u32[]{:S(2)}) copy-start(f32[512,128]{1,0:T(8,128)} %damp_any.1) | copy-start | bytes 786436
  4.0 0.7 %copy-start.2 = (s32[4096]{0:T(1024)S(1)}, s32[4096]{0:T(1024)}, u32[]{:S(2)}) copy-start(s32[4096]{0:T(1024)} %param.9) | copy-start | bytes 49156
  4.7 0.7 %copy-start.3 = (s32[16,16]{1,0:T(8,128)S(1)}, s32[16,16]{1,0:T(8,128)}, u32[]{:S(2)}) copy-start(s32[16,16]{1,0:T(8,128)} %foot_ref.1) | copy-start | bytes 3076
  5.4 0.7 %copy-start.4 = (f32[16]{0:T(128)S(1)}, f32[16]{0:T(128)}, u32[]{:S(2)}) copy-start(f32[16]{0:T(128)} %w_ref.1) | copy-start | bytes 196
  6.0 0.7 %copy-start.5 = (f32[8]{0:T(128)S(1)}, f32[8]{0:T(128)}, u32[]{:S(2)}) copy-start(f32[8]{0:T(128)} %len_ref.1) | copy-start | bytes 100

commit v2 on v1

--- a/solution.py
+++ b/solution.py
@@ -11,6 +11,7 @@
 F32, BF16, I32 = jnp.float32, jnp.bfloat16, jnp.int32
 LANES = 128
 PIECES = 4
+VMEM_BYTES = 63 * 1024 * 1024
 
 
 def count(shape, dim):
@@ -41,11 +42,11 @@
 
 def kernel(
     sizes,
-    jac_any, foot_ref, home_ref, res_ref, w_ref, damp_any, len_ref,
-    step_any, change_ref, curve_ref,
-    jac, damp, terms, other, split, pick, pick_t, slot_out, slot_in, put, put_t,
+    jac_any, foot_any, home_any, res_any, w_any, damp_any, len_any,
+    step_any, change_any, curve_any,
+    jac, foot_ref, home_ref, res_ref, w_ref, len_ref, change_ref, curve_ref, damp, terms, other, split, pick, pick_t, slot_out, slot_in, put, put_t,
     out, inn, both, step, low, rep, ret, entry, curves,
-    load_sem, damp_sem, step_sem, pair_sem, total_sem, slot_sem, out_sem, rep_sem, curve_sem,
+    load_sem, small_sem, store_sem, pair_sem, total_sem, slot_sem, out_sem, rep_sem, curve_sem,
 ):
     n, groups, cap, sites, foot, freqs, comps, blocks = sizes
     entries = sites * foot
@@ -61,7 +62,7 @@
         def one(j, carry):
             body((me + j) % n)
             return carry
-        lax.fori_loop(1, n, one, 0)
+        lax.fori_loop(1, n, one, 0, unroll=n <= 16)
 
     def place(o):
         return pl.ds(pl.multiple_of(o * cap, cap), cap)
@@ -72,6 +73,21 @@
             device_id=to, device_id_type=MESH,
         )
 
+    small = [
+        pltpu.make_async_copy(source, target, small_sem.at[i])
+        for i, (source, target) in enumerate(
+            (
+                (foot_any, foot_ref),
+                (home_any, home_ref),
+                (res_any, res_ref),
+                (w_any, w_ref),
+                (len_any, len_ref),
+                (damp_any, damp),
+            )
+        )
+    ]
+    for load in small:
+        load.start()
     piece = entries // PIECES
     loads = [
         pltpu.make_async_copy(
@@ -81,13 +97,40 @@
     ]
     for load in loads:
         load.start()
-    damp_load = pltpu.make_async_copy(damp_any, damp, damp_sem)
-    damp_load.start()
     barrier = pltpu.get_barrier_semaphore()
     pl.semaphore_signal(barrier, inc=1, device_id=partner, device_id_type=MESH)
     others(
         lambda o: pl.semaphore_signal(barrier, inc=1, device_id=at(o), device_id_type=MESH)
     )
+
+    for load in small[:-1]:
+        load.wait()
+
+
+    def pair_copy(c):
+        span = pl.ds(c * piece, piece)
+        return remote(terms.at[1 - freq, span], other.at[span], pair_sem, c, c, partner)
+
+    site_lane = count((freqs * comps, sites), 1)
+    w_row = w_ref[...]
+    residual = res_ref[...].reshape(freqs * comps, sites)
+    weighted = (residual * w_row).astype(BF16).astype(F32)
+
+    def site_terms(s, carry):
+        col = jnp.sum(jnp.where(site_lane == s, weighted, 0.0), axis=1, keepdims=True)
+        w = jnp.sum(jnp.where(site_lane[:1] == s, w_row, 0.0), axis=1, keepdims=True)
+        span = pl.ds(pl.multiple_of(s * foot, foot), foot)
+        j = jac[span].astype(F32)
+        terms[0, span, :] = jnp.sum(j * col[None], axis=1)
+        terms[1, span, :] = jnp.sum(j * j, axis=1) * w
+        return carry
+
+    for c in range(PIECES):
+        loads[c].wait()
+        lax.fori_loop(c * sites // PIECES, (c + 1) * sites // PIECES, site_terms, 0, unroll=2)
+        if c == 0:
+            pl.semaphore_wait(barrier, n)
+        pair_copy(c).start()
 
     block = jnp.concatenate(
         [column_of(foot_ref[s : s + 1, :].astype(F32), foot) for s in range(sites)], axis=0
@@ -122,36 +165,10 @@
     lax.fori_loop(0, n, list_slots, 0)
     slot_in[me] = slot_out[me]
 
-    pl.semaphore_wait(barrier, n)
-
     def slot_copy(o, source):
         return remote(slot_out.at[o], slot_in.at[source], slot_sem, o, source, at(o))
 
     others(lambda o: slot_copy(o, me).start())
-
-    def pair_copy(c):
-        span = pl.ds(c * piece, piece)
-        return remote(terms.at[1 - freq, span], other.at[span], pair_sem, c, c, partner)
-
-    def site_terms(s, carry):
-        w = w_ref[s]
-        weighted = jnp.concatenate(
-            [
-                column_of((res_ref[s, f : f + 1, :] * w).astype(BF16).astype(F32), comps)
-                for f in range(freqs)
-            ],
-            axis=0,
-        )
-        span = pl.ds(pl.multiple_of(s * foot, foot), foot)
-        j = jac[span].astype(F32)
-        terms[0, span, :] = jnp.sum(j * weighted[None], axis=1)
-        terms[1, span, :] = jnp.sum(j * j, axis=1) * w
-        return carry
-
-    for c in range(PIECES):
-        loads[c].wait()
-        lax.fori_loop(c * sites // PIECES, (c + 1) * sites // PIECES, site_terms, 0)
-        pair_copy(c).start()
     for c in range(PIECES):
         span = pl.ds(c * piece, piece)
         pair_copy(c).wait_recv()
@@ -160,18 +177,13 @@
         split[span, :LANES] = high
         split[span, LANES:] = (t - high.astype(F32)).astype(BF16)
 
-    def bucket_rows(o):
-        return dot(pick[place(o), :], split[...]).astype(BF16)
+    out[...] = dot(pick[...], split[...]).astype(BF16)
 
     def out_copy(o, source):
-        return remote(out.at[o], inn.at[place(source)], out_sem, o, source, at(o))
-
-    def send_out(o):
-        out[o] = bucket_rows(o)
-        out_copy(o, me).start()
-
-    others(send_out)
-    inn[place(me), :] = bucket_rows(me)
+        return remote(out.at[place(o)], inn.at[place(source)], out_sem, o, source, at(o))
+
+    others(lambda o: out_copy(o, me).start())
+    inn[place(me), :] = out[place(me), :]
 
     others(lambda o: slot_copy(o, o).wait_recv())
     per = LANES // cap
@@ -196,60 +208,46 @@
         t = dot(put[c * part : (c + 1) * part, :], inn[...])
         both[freq, pl.ds(c * part, part), :] = t[:, :LANES] + t[:, LANES:]
         total_copy(c).start()
-    damp_load.wait()
+    small[-1].wait()
     for c in range(PIECES):
         span = pl.ds(c * part, part)
         total_copy(c).wait_recv()
         update = both[0, span, :] / (both[1, span, :] + damp[span, :])
         step[span, :] = update
         low[span, :] = update.astype(BF16)
-    step_store = pltpu.make_async_copy(step, step_any, step_sem)
+    step_store = pltpu.make_async_copy(step, step_any, store_sem.at[0])
     step_store.start()
 
-    def reply_rows(o):
-        return dot(put_t[place(o), :], low[...]).astype(BF16)
+    rep[...] = dot(put_t[...], low[...]).astype(BF16)
 
     def rep_copy(o, source):
-        return remote(rep.at[o], ret.at[place(source)], rep_sem, o, source, at(o))
-
-    def send_reply(o):
-        rep[o] = reply_rows(o)
-        rep_copy(o, me).start()
-
-    others(send_reply)
-    ret[place(me), :] = reply_rows(me)
+        return remote(rep.at[place(o)], ret.at[place(source)], rep_sem, o, source, at(o))
+
+    others(lambda o: rep_copy(o, me).start())
+    ret[place(me), :] = rep[place(me), :]
     others(lambda o: rep_copy(o, o).wait_recv())
     entry[...] = dot(pick_t[...], ret[...])
 
-    steps = len_ref.shape[0]
-    eye = diagonal(comps, LANES)
-
-    def site_change(s, sums):
+    steps = len_ref.shape[1]
+
+    def site_change(s, change):
         acc = jnp.zeros((freqs * comps, LANES), F32)
         for k in range(foot):
             e = s * foot + k
             acc = acc + jac[e].astype(F32) * entry[pl.ds(e, 1), :]
         total = jnp.sum(acc, axis=1, keepdims=True)
-        ch = jnp.concatenate(
-            [
-                jnp.sum(
-                    jnp.where(eye, total[f * comps : (f + 1) * comps], 0.0), axis=0, keepdims=True
-                )
-                for f in range(freqs)
-            ],
-            axis=0,
-        )[:, :comps]
-        change_ref[s] = ch
-        r, w = res_ref[s], w_ref[s]
-        gaps = [r - len_ref[a] * ch for a in range(steps)]
-        return tuple(t + w * (g * g) for t, g in zip(sums, gaps))
-
-    zero = jnp.zeros((freqs, comps), F32)
-    sums = lax.fori_loop(0, sites, site_change, (zero,) * steps)
+        return jnp.where(site_lane == s, total, change)
+
+    change = lax.fori_loop(0, sites, site_change, jnp.zeros((freqs * comps, sites), F32), unroll=4)
+    change_ref[...] = change.reshape(freqs, comps, sites)
+    change_store = pltpu.make_async_copy(change_ref, change_any, store_sem.at[1])
+    change_store.start()
     mine = jnp.zeros((freqs, LANES), F32)
     for a in range(steps):
-        here = count((freqs, LANES), 1) == a
-        mine = mine + jnp.where(here, jnp.sum(sums[a], axis=1, keepdims=True), 0.0)
+        gap = residual - len_ref[0:1, a : a + 1] * change
+        lost = (w_row * (gap * gap)).reshape(freqs, comps, sites)
+        lost = jnp.sum(jnp.sum(lost, axis=1), axis=1, keepdims=True)
+        mine = mine + jnp.where(count((freqs, LANES), 1) == a, lost, 0.0)
     curves[me] = jnp.zeros((8, LANES), F32)
     curves[me, :freqs, :] = mine
 
@@ -263,6 +261,8 @@
     )
     curve_ref[...] = total[:freqs, :steps] * (1.0 / (n * sites * comps))
 
+    curve_store = pltpu.make_async_copy(curve_ref, curve_any, store_sem.at[2])
+    curve_store.start()
     for c in range(PIECES):
         pair_copy(c).wait_send()
         total_copy(c).wait_send()
@@ -271,6 +271,8 @@
     others(lambda o: rep_copy(o, me).wait_send())
     others(lambda o: curve_copy(o, me).wait_send())
     step_store.wait()
+    change_store.wait()
+    curve_store.wait()
 
 
 def shards(jacobian, footprint, home, residual, weights, damping, step_lengths):
@@ -284,21 +286,26 @@
         cap *= 2
     rows = n * cap
     sizes = (n, groups, cap, sites, foot, freqs, comps, blocks)
-    vmem = pl.BlockSpec(memory_space=pltpu.VMEM)
-    smem = pl.BlockSpec(memory_space=pltpu.SMEM)
     hbm = pl.BlockSpec(memory_space=pl.ANY)
     dma = pltpu.SemaphoreType.DMA
-    return pl.pallas_call(
+    model_step, change, curve = pl.pallas_call(
         functools.partial(kernel, sizes),
         out_shape=(
             jax.ShapeDtypeStruct((blocks, width), F32),
-            jax.ShapeDtypeStruct((sites, freqs, comps), F32),
+            jax.ShapeDtypeStruct((freqs, comps, sites), F32),
             jax.ShapeDtypeStruct((freqs, step_lengths.shape[0]), F32),
         ),
-        in_specs=[hbm, vmem, vmem, vmem, smem, hbm, smem],
-        out_specs=(hbm, vmem, vmem),
+        in_specs=[hbm] * 7,
+        out_specs=(hbm,) * 3,
         scratch_shapes=[
             pltpu.VMEM((entries, freqs * comps, width), BF16),
+            pltpu.VMEM((sites, foot), I32),
+            pltpu.VMEM((home.shape[0] // LANES, LANES), I32),
+            pltpu.VMEM((freqs, comps, sites), F32),
+            pltpu.VMEM((1, sites), F32),
+            pltpu.VMEM((1, step_lengths.shape[0]), F32),
+            pltpu.VMEM((freqs, comps, sites), F32),
+            pltpu.VMEM((freqs, step_lengths.shape[0]), F32),
             pltpu.VMEM((blocks, width), F32),
             pltpu.VMEM((2, entries, width), F32),
             pltpu.VMEM((entries, width), F32),
@@ -309,18 +316,18 @@
             pltpu.VMEM((n, 8, LANES), F32),
             pltpu.VMEM((blocks, rows), BF16),
             pltpu.VMEM((rows, blocks), BF16),
-            pltpu.VMEM((n, cap, 2 * width), BF16),
+            pltpu.VMEM((rows, 2 * width), BF16),
             pltpu.VMEM((rows, 2 * width), BF16),
             pltpu.VMEM((2, blocks, width), F32),
             pltpu.VMEM((blocks, width), F32),
             pltpu.VMEM((blocks, width), BF16),
-            pltpu.VMEM((n, cap, width), BF16),
+            pltpu.VMEM((rows, width), BF16),
             pltpu.VMEM((rows, width), BF16),
             pltpu.VMEM((entries, width), F32),
             pltpu.VMEM((n, 8, LANES), F32),
             dma((PIECES,)),
-            dma,
-            dma,
+            dma((6,)),
+            dma((3,)),
             dma((2, PIECES)),
             dma((2, PIECES)),
             dma((2, n)),
@@ -329,17 +336,18 @@
             dma((2, n)),
         ],
         compiler_params=pltpu.CompilerParams(
-            collective_id=0, has_side_effects=True, vmem_limit_bytes=48 * 1024 * 1024
+            collective_id=0, has_side_effects=True, vmem_limit_bytes=VMEM_BYTES
         ),
     )(
         jacobian.reshape(entries, freqs * comps, width),
         footprint,
         home.reshape(-1, LANES),
-        residual,
-        weights,
+        residual.transpose(1, 2, 0),
+        weights.reshape(1, -1),
         damping,
-        step_lengths,
-    )
+        step_lengths.reshape(1, -1),
+    )
+    return model_step, change.transpose(2, 0, 1), curve
 
 
 def solution(mesh):

time: 42.7 us -> 35.4 us (0.83)
  local copies, waits for them, and re-layouts: 8.03 us -> 4.25 us
  Pallas kernels: 33.7 us -> 30.1 us
    pallas_call x1, Pallas kernels: 33.7 us -> 30.1 us  [shards(): pl.pallas_call(functools.partial(kernel, sizes), out_shape=(jax.ShapeDtyp...]
    unnamed x15 -> x3, local copies, waits for them, and re-layouts: 7.34 us -> 4.25 us
    pallas_call x1 -> x0, local copies, waits for them, and re-layouts: 0.68 us -> none  [shards(): pl.pallas_call(functools.partial(kernel, sizes), out_shape=(jax.ShapeDtyp...]
where the time goes in v2:
time: 35.4 us; the launch traced here: 35 us
  Pallas kernels  30.1 us (85%)
  local copies, waits for them, and re-layouts  4.25 us (12%)
  between operations  0.64 us (2%)
    pallas_call x1, Pallas kernels, shards(): pl.pallas_call(functools.partial(kernel, sizes), out_shape=(jax.ShapeDtyp...  30.1 us
    unnamed x3, local copies, waits for them, and re-layouts  4.25 us

profile of v2, /device:TPU:0, one launch (start us, length us, event | category | flops | bytes accessed | tf_op | source)
XLA Modules:
  0.0 35.0 jit_solution(17283179018649089260)
XLA Ops:
  0.6 30.1 %shard_map.94 = (f32[512,128]{1,0:T(8,128)}, f32[4,8,16]{2,1,0:T(8,128)}, f32[4,8]{1,0:T(4,128)}) custom-call(bf16[256,32,128]{2,1,0:T(8,128)(2,1)} %bitcast.6, s32[16,16]{1,0:T(8,128)} %foot_any.1, s32[32,128]{1,0:T(8,128)} %bitcast.7, f32[4,8,16]{2,1,0:T(8,128)} %bitcast.8, f32[1,16]{1,0:T(1,128)} %bitcast.10, f32[512,128]{1,0:T(8,128)} %damp_any.1, ...), custom_call_target="tpu_custom_call" | custom-call | tf_op jit(solution)/shard_map/pallas_call | solution.py:291
  30.8 1.7 %copy.13 = f32[512,128]{1,0:T(8,128)} copy(f32[512,128]{1,0:T(8,128)} %get-tuple-element.12) | data formatting | bytes 524288
  32.4 1.3 %copy.14 = f32[16,4,8]{0,2,1:T(8,128)} copy(f32[16,4,8]{0,2,1:T(8,128)} %bitcast.9) | data formatting | bytes 4096
  33.8 1.3 %copy.15 = f32[4,8]{1,0:T(4,128)} copy(f32[4,8]{1,0:T(4,128)} %get-tuple-element.14) | data formatting | bytes 256

commit v3 on v2

--- a/solution.py
+++ b/solution.py
@@ -11,7 +11,7 @@
 F32, BF16, I32 = jnp.float32, jnp.bfloat16, jnp.int32
 LANES = 128
 PIECES = 4
-VMEM_BYTES = 63 * 1024 * 1024
+VMEM_BYTES = 32 * 1024 * 1024
 
 
 def count(shape, dim):
@@ -43,10 +43,10 @@
 def kernel(
     sizes,
     jac_any, foot_any, home_any, res_any, w_any, damp_any, len_any,
-    step_any, change_any, curve_any,
-    jac, foot_ref, home_ref, res_ref, w_ref, len_ref, change_ref, curve_ref, damp, terms, other, split, pick, pick_t, slot_out, slot_in, put, put_t,
-    out, inn, both, step, low, rep, ret, entry, curves,
-    load_sem, small_sem, store_sem, pair_sem, total_sem, slot_sem, out_sem, rep_sem, curve_sem,
+    step, change_ref, curve_ref,
+    jac, foot_ref, home_ref, res_ref, w_ref, len_ref, damp, terms, other, split, pick, pick_t, slot_out, slot_in, put, put_t,
+    out, inn, both, low, rep, ret, entry, curves,
+    load_sem, small_sem, pair_sem, total_sem, slot_sem, out_sem, rep_sem, curve_sem,
 ):
     n, groups, cap, sites, foot, freqs, comps, blocks = sizes
     entries = sites * foot
@@ -128,9 +128,6 @@
     for c in range(PIECES):
         loads[c].wait()
         lax.fori_loop(c * sites // PIECES, (c + 1) * sites // PIECES, site_terms, 0, unroll=2)
-        if c == 0:
-            pl.semaphore_wait(barrier, n)
-        pair_copy(c).start()
 
     block = jnp.concatenate(
         [column_of(foot_ref[s : s + 1, :].astype(F32), foot) for s in range(sites)], axis=0
@@ -165,6 +162,10 @@
     lax.fori_loop(0, n, list_slots, 0)
     slot_in[me] = slot_out[me]
 
+    pl.semaphore_wait(barrier, n)
+    for c in range(PIECES):
+        pair_copy(c).start()
+
     def slot_copy(o, source):
         return remote(slot_out.at[o], slot_in.at[source], slot_sem, o, source, at(o))
 
@@ -215,8 +216,6 @@
         update = both[0, span, :] / (both[1, span, :] + damp[span, :])
         step[span, :] = update
         low[span, :] = update.astype(BF16)
-    step_store = pltpu.make_async_copy(step, step_any, store_sem.at[0])
-    step_store.start()
 
     rep[...] = dot(put_t[...], low[...]).astype(BF16)
 
@@ -240,8 +239,6 @@
 
     change = lax.fori_loop(0, sites, site_change, jnp.zeros((freqs * comps, sites), F32), unroll=4)
     change_ref[...] = change.reshape(freqs, comps, sites)
-    change_store = pltpu.make_async_copy(change_ref, change_any, store_sem.at[1])
-    change_store.start()
     mine = jnp.zeros((freqs, LANES), F32)
     for a in range(steps):
         gap = residual - len_ref[0:1, a : a + 1] * change
@@ -261,8 +258,6 @@
     )
     curve_ref[...] = total[:freqs, :steps] * (1.0 / (n * sites * comps))
 
-    curve_store = pltpu.make_async_copy(curve_ref, curve_any, store_sem.at[2])
-    curve_store.start()
     for c in range(PIECES):
         pair_copy(c).wait_send()
         total_copy(c).wait_send()
@@ -270,9 +265,18 @@
     others(lambda o: out_copy(o, me).wait_send())
     others(lambda o: rep_copy(o, me).wait_send())
     others(lambda o: curve_copy(o, me).wait_send())
-    step_store.wait()
-    change_store.wait()
-    curve_store.wait()
+
+
+def store(*refs):
+    count = len(refs) // 2
+    sems = refs[-1]
+    copies = [
+        pltpu.make_async_copy(refs[i], refs[count + i], sems.at[i]) for i in range(count)
+    ]
+    for copy in copies:
+        copy.start()
+    for copy in copies:
+        copy.wait()
 
 
 def shards(jacobian, footprint, home, residual, weights, damping, step_lengths):
@@ -286,9 +290,11 @@
         cap *= 2
     rows = n * cap
     sizes = (n, groups, cap, sites, foot, freqs, comps, blocks)
-    hbm = pl.BlockSpec(memory_space=pl.ANY)
+    hbm = pl.BlockSpec(memory_space=pltpu.HBM)
+    free = pl.BlockSpec(memory_space=pl.ANY)
+    vmem = pl.BlockSpec(memory_space=pltpu.VMEM)
     dma = pltpu.SemaphoreType.DMA
-    model_step, change, curve = pl.pallas_call(
+    results = pl.pallas_call(
         functools.partial(kernel, sizes),
         out_shape=(
             jax.ShapeDtypeStruct((blocks, width), F32),
@@ -296,7 +302,7 @@
             jax.ShapeDtypeStruct((freqs, step_lengths.shape[0]), F32),
         ),
         in_specs=[hbm] * 7,
-        out_specs=(hbm,) * 3,
+        out_specs=(vmem,) * 3,
         scratch_shapes=[
             pltpu.VMEM((entries, freqs * comps, width), BF16),
             pltpu.VMEM((sites, foot), I32),
@@ -304,8 +310,6 @@
             pltpu.VMEM((freqs, comps, sites), F32),
             pltpu.VMEM((1, sites), F32),
             pltpu.VMEM((1, step_lengths.shape[0]), F32),
-            pltpu.VMEM((freqs, comps, sites), F32),
-            pltpu.VMEM((freqs, step_lengths.shape[0]), F32),
             pltpu.VMEM((blocks, width), F32),
             pltpu.VMEM((2, entries, width), F32),
             pltpu.VMEM((entries, width), F32),
@@ -319,7 +323,6 @@
             pltpu.VMEM((rows, 2 * width), BF16),
             pltpu.VMEM((rows, 2 * width), BF16),
             pltpu.VMEM((2, blocks, width), F32),
-            pltpu.VMEM((blocks, width), F32),
             pltpu.VMEM((blocks, width), BF16),
             pltpu.VMEM((rows, width), BF16),
             pltpu.VMEM((rows, width), BF16),
@@ -327,7 +330,6 @@
             pltpu.VMEM((n, 8, LANES), F32),
             dma((PIECES,)),
             dma((6,)),
-            dma((3,)),
             dma((2, PIECES)),
             dma((2, PIECES)),
             dma((2, n)),
@@ -339,14 +341,27 @@
             collective_id=0, has_side_effects=True, vmem_limit_bytes=VMEM_BYTES
         ),
     )(
-        jacobian.reshape(entries, freqs * comps, width),
-        footprint,
-        home.reshape(-1, LANES),
-        residual.transpose(1, 2, 0),
-        weights.reshape(1, -1),
-        damping,
-        step_lengths.reshape(1, -1),
-    )
+        *(
+            pltpu.with_memory_space_constraint(x, pltpu.HBM)
+            for x in (
+                jacobian.reshape(entries, freqs * comps, width),
+                footprint,
+                home.reshape(-1, LANES),
+                residual.transpose(1, 2, 0),
+                weights.reshape(1, -1),
+                damping,
+                step_lengths.reshape(1, -1),
+            )
+        )
+    )
+    model_step, change, curve = pl.pallas_call(
+        store,
+        out_shape=tuple(jax.ShapeDtypeStruct(r.shape, r.dtype) for r in results),
+        in_specs=[free] * len(results),
+        out_specs=(hbm,) * len(results),
+        scratch_shapes=[dma((len(results),))],
+        compiler_params=pltpu.CompilerParams(vmem_limit_bytes=VMEM_BYTES // 8),
+    )(*results)
     return model_step, change.transpose(2, 0, 1), curve
 
 

time: 35.4 us -> 31.1 us (0.88)
  local copies, waits for them, and re-layouts: 4.25 us -> 0 us
    unnamed x3 -> x0, local copies, waits for them, and re-layouts: 4.25 us -> none
    pallas_call x0 -> x1, Pallas kernels: none -> 0.74 us  [shards(): pl.pallas_call(store, out_shape=tuple((jax.ShapeDtypeStruct(r.shape, r.dt...]
    pallas_call x1, Pallas kernels: 30.1 us -> 29.5 us  [shards(): pl.pallas_call(functools.partial(kernel, sizes), out_shape=(jax.ShapeDtyp...]
where the time goes in v3:
time: 31.1 us; the launch traced here: 30.8 us
  Pallas kernels  30.2 us (97%)
  between operations  0.64 us (2%)
    pallas_call x1, Pallas kernels, shards(): pl.pallas_call(functools.partial(kernel, sizes), out_shape=(jax.ShapeDtyp...  29.5 us
    pallas_call x1, Pallas kernels, shards(): pl.pallas_call(store, out_shape=tuple((jax.ShapeDtypeStruct(r.shape, r.dt...  0.74 us

profile of v3, /device:TPU:0, one launch (start us, length us, event | category | flops | bytes accessed | tf_op | source)
XLA Modules:
  0.0 30.8 jit_solution(3979144130322464212)
XLA Ops:
  0.6 29.5 %shard_map.94 = (f32[512,128]{1,0:T(8,128)S(1)}, f32[4,8,16]{2,1,0:T(8,128)S(1)}, f32[4,8]{1,0:T(4,128)S(1)}) custom-call(bf16[256,32,128]{2,1,0:T(8,128)(2,1)} %bitcast.6, s32[16,16]{1,0:T(8,128)} %foot_any.1, s32[32,128]{1,0:T(8,128)} %bitcast.7, f32[4,8,16]{2,1,0:T(8,128)} %bitcast.8, f32[1,16]{1,0:T(1,128)} %bitcast.9, f32[512,128]{1,0:T(8,128)} %damp_any.1, ...), custom_call_target="tpu_custom_call" | custom-call | tf_op jit(solution)/shard_map/pallas_call | solution.py:297
  30.1 0.7 %shard_map.95 = (f32[512,128]{1,0:T(8,128)}, f32[4,8,16]{2,1,0:T(8,128)}, f32[4,8]{1,0:T(4,128)}) custom-call(f32[512,128]{1,0:T(8,128)S(1)} %get-tuple-element.9.refs_0_, f32[4,8,16]{2,1,0:T(8,128)S(1)} %get-tuple-element.10.refs_1_, f32[4,8]{1,0:T(4,128)S(1)} %get-tuple-element.11.refs_2_), custom_call_target="tpu_custom_call" | custom-call | tf_op jit(solution)/shard_map/pallas_call | solution.py:357

commit v4 on v3

--- a/solution.py
+++ b/solution.py
@@ -62,7 +62,11 @@
         def one(j, carry):
             body((me + j) % n)
             return carry
-        lax.fori_loop(1, n, one, 0, unroll=n <= 16)
+        if n > 16:
+            lax.fori_loop(1, n, one, 0)
+        else:
+            for j in sorted(range(1, n), key=lambda j: abs(2 * j - n)):
+                one(j, 0)
 
     def place(o):
         return pl.ds(pl.multiple_of(o * cap, cap), cap)

time: 31.1 us -> 32 us (1.029)
  Pallas kernels: 30.2 us -> 31.1 us
    pallas_call x1, Pallas kernels: 29.5 us -> 30.4 us  [shards(): pl.pallas_call(functools.partial(kernel, sizes), out_shape=(jax.ShapeDtyp...]
where the time goes in v4:
time: 32 us; the launch traced here: 31.7 us
  Pallas kernels  31.1 us (97%)
  between operations  0.64 us (2%)
    pallas_call x1, Pallas kernels, shards(): pl.pallas_call(functools.partial(kernel, sizes), out_shape=(jax.ShapeDtyp...  30.4 us
    pallas_call x1, Pallas kernels, shards(): pl.pallas_call(store, out_shape=tuple((jax.ShapeDtypeStruct(r.shape, r.dt...  0.74 us

profile of v4, /device:TPU:0, one launch (start us, length us, event | category | flops | bytes accessed | tf_op | source)
XLA Modules:
  0.0 31.7 jit_solution(2663937443937034617)
XLA Ops:
  0.6 30.4 %shard_map.94 = (f32[512,128]{1,0:T(8,128)S(1)}, f32[4,8,16]{2,1,0:T(8,128)S(1)}, f32[4,8]{1,0:T(4,128)S(1)}) custom-call(bf16[256,32,128]{2,1,0:T(8,128)(2,1)} %bitcast.6, s32[16,16]{1,0:T(8,128)} %foot_any.1, s32[32,128]{1,0:T(8,128)} %bitcast.7, f32[4,8,16]{2,1,0:T(8,128)} %bitcast.8, f32[1,16]{1,0:T(1,128)} %bitcast.9, f32[512,128]{1,0:T(8,128)} %damp_any.1, ...), custom_call_target="tpu_custom_call" | custom-call | tf_op jit(solution)/shard_map/pallas_call | solution.py:301
  31.0 0.7 %shard_map.95 = (f32[512,128]{1,0:T(8,128)}, f32[4,8,16]{2,1,0:T(8,128)}, f32[4,8]{1,0:T(4,128)}) custom-call(f32[512,128]{1,0:T(8,128)S(1)} %get-tuple-element.9.refs_0_, f32[4,8,16]{2,1,0:T(8,128)S(1)} %get-tuple-element.10.refs_1_, f32[4,8]{1,0:T(4,128)S(1)} %get-tuple-element.11.refs_2_), custom_call_target="tpu_custom_call" | custom-call | tf_op jit(solution)/shard_map/pallas_call | solution.py:361
